TPU v7x, 32 devices: a whole 2x2x4 slice. The times are simulated.
32 devices in a mesh: samp: 8 (over z, y), feat: 4 (over x, core).
Axes of the slice: x: 2, y: 2, z: 4, core: 2. Of those that a mesh axis runs over, the one named last changes fastest.
Arguments:
- states: bfloat16 [8192, 16384], P('samp', 'feat'), may hold values from -0.176776695 to 0.176776695
- targets: float32 [8192, 128], P('samp'), may hold values from -40 to 40
- penalty: float32 [128], replicated, may hold values from 0.1 to 1
Outputs:
- readout: float32 [16384, 128], P('feat')
- residual: float32 [8192, 128], P('samp')
All inputs are finite; a program needn't handle non-finite values.
Results may differ from a plain program's by a relative error of at most 0.0058.
Values may be sent and summed in bfloat16 or wider, within the bound.
A program may use at most 64 MiB of HBM per device.

v0:
```python
import jax
import jax.numpy as jnp
from jax import lax
from jax.sharding import PartitionSpec as P

ITERS = 3


def shards(states, targets, penalty):
    feat_rows = states.shape[1]

    def weight_sum(value):
        return lax.psum(value, "feat")

    def gradient_of(residual, readout):
        residual_b = residual.astype(jnp.bfloat16)
        partial_value = lax.dot_general(
            states, residual_b, (((0,), (0,)), ((), ())), preferred_element_type=jnp.float32
        )
        summed = lax.psum(partial_value, "samp")
        return summed - penalty * readout

    readout = jnp.zeros((feat_rows, targets.shape[1]), jnp.float32)
    residual = targets
    gradient = gradient_of(residual, readout)
    direction = gradient
    norm_now = weight_sum(jnp.sum(gradient * gradient, axis=0))
    for step in range(ITERS):
        direction_b = direction.astype(jnp.bfloat16)
        image_partial_value = jnp.dot(states, direction_b, preferred_element_type=jnp.float32)
        image = lax.psum(image_partial_value, "feat")
        image_sq = jnp.sum(image * image, axis=0)
        direction_sq = jnp.sum(direction * direction, axis=0)
        curvature = lax.psum(image_sq, "samp") + penalty * weight_sum(direction_sq)
        step_size = norm_now / curvature
        readout = readout + step_size * direction
        residual = residual - step_size * image
        if step + 1 < ITERS:
            gradient = gradient_of(residual, readout)
            norm_next = weight_sum(jnp.sum(gradient * gradient, axis=0))
            direction = gradient + norm_next / norm_now * direction
            norm_now = norm_next
    return (readout, residual)


def solution(mesh):
    in_specs = (P("samp", "feat"), P("samp", None), P())
    out_specs = (P("feat", None), P("samp", None))
    return jax.shard_map(shards, mesh=mesh, in_specs=in_specs, out_specs=out_specs, check_vma=False)
```

profile of v0, /device:TPU:0, one launch (start us, length us, event | category | flops | bytes accessed | tf_op | source)
XLA Modules:
  0.0 558.5 jit_solution(16675980969986547672)
XLA Ops:
  7.2 0.0 all-reduce.7.cloned.1.call-start
  7.2 7.1 %fusion.5 = f32[4096,128]{1,0:T(8,128)} fusion(bf16[1024,4096]{1,0:T(8,128)(2,1)} %param.3, f32[1024,128]{1,0:T(8,128)} %param.4), kind=kOutput, calls=%fused_computation.28 | convolution fusion | flops 1073872896 | bytes 11010048 | tf_op jit(solution)/shard_map/dot_general | solution.py:17
  14.3 0.0 all-reduce.7.cloned.1.call-update
  14.4 0.0 all-reduce.9.cloned.1.call-start
  14.4 0.6 copy-done.6
  15.0 104.0 %all-reduce.7.cloned.1.call-done = f32[4096,128]{1,0:T(8,128)} async-done(((f32[4096,128]{1,0:T(8,128)}), f32[4096,128]{1,0:T(8,128)}) %all-reduce.7.cloned.1.call-update) | async-done | bytes 2097168 | tf_op jit(solution)/shard_map/psum | solution.py:20
  119.0 7.8 %convolution_bitcast_fusion.4 = f32[1024,128]{0,1:T(8,128)} fusion(bf16[1024,4096]{1,0:T(8,128)(2,1)} %param.3, f32[4096,128]{1,0:T(8,128)} %all-reduce.7.cloned.1.call-done, f32[128]{0:T(128)S(1)} %broadcast_multiply_fusion), kind=kOutput, calls=%fused_computation.16 | convolution fusion | flops 1074790400 | bytes 11010560 | tf_op jit(solution)/shard_map/dot_general | solution.py:30
  126.9 0.0 all-reduce.9.cloned.1.call-update
  126.9 0.0 all-reduce.11.cloned.1.call-start
  126.9 0.2 copy.5
  127.2 0.6 multiply_reduce_fusion.4
  127.7 6.3 %psum.102 = f32[128]{0:T(128)S(1)} all-reduce(f32[128]{0:T(128)S(1)} %multiply_reduce_fusion.4), channel_id=1, replica_groups=mesh['samp'=8,'feat'=4] {'feat'}, use_global_device_ids=true, to_apply=%region_2.0 | all-reduce | flops 128 | bytes 1024 | tf_op jit(solution)/shard_map/psum | solution.py:13
  134.0 25.9 %all-reduce.9.cloned.1.call-done = f32[1024,128]{0,1:T(8,128)} async-done(((f32[1024,128]{0,1:T(8,128)}), f32[1024,128]{0,1:T(8,128)}) %all-reduce.9.cloned.1.call-update) | async-done | bytes 524304 | tf_op jit(solution)/shard_map/psum | solution.py:31
  159.9 1.2 multiply_reduce_fusion.7
  161.1 21.4 %psum.104 = f32[128]{0:T(128)S(1)} all-reduce(f32[128]{0:T(128)S(1)} %multiply_reduce_fusion.7), channel_id=1, replica_groups=mesh['samp'=8,'feat'=4] {'samp'}, use_global_device_ids=true, to_apply=%region_5.0 | all-reduce | flops 128 | bytes 1024 | tf_op jit(solution)/shard_map/psum | solution.py:34
  182.5 8.3 %convolution_bitcast_fusion.1 = f32[4096,128]{1,0:T(8,128)} fusion(bf16[1024,4096]{1,0:T(8,128)(2,1)} %param.3, f32[1024,128]{0,1:T(8,128)S(1)} %copy.5, f32[1024,128]{0,1:T(8,128)} %all-reduce.9.cloned.1.call-done, f32[128]{0:T(128)S(1)} %add_divide_fusion.2), kind=kOutput, calls=%fused_computation.1 | convolution fusion | flops 1074135040 | bytes 11534848 | tf_op jit(solution)/shard_map/dot_general | solution.py:17
  190.8 0.0 all-reduce.11.cloned.1.call-update
  190.8 0.0 all-reduce.13.cloned.1.call-start
  190.8 98.2 %all-reduce.11.cloned.1.call-done = f32[4096,128]{1,0:T(8,128)} async-done(((f32[4096,128]{1,0:T(8,128)}), f32[4096,128]{1,0:T(8,128)}) %all-reduce.11.cloned.1.call-update) | async-done | bytes 2097168 | tf_op jit(solution)/shard_map/psum | solution.py:20
  289.0 2.2 multiply_reduce_fusion.3
  291.1 6.5 %psum.106 = f32[128]{0:T(128)S(1)} all-reduce(f32[128]{0:T(128)S(1)} %multiply_reduce_fusion.3), channel_id=1, replica_groups=mesh['samp'=8,'feat'=4] {'feat'}, use_global_device_ids=true, to_apply=%region_8.0 | all-reduce | flops 128 | bytes 1024 | tf_op jit(solution)/shard_map/psum | solution.py:13
  297.6 7.7 %convolution_bitcast_fusion.3 = f32[1024,128]{0,1:T(8,128)} fusion(bf16[1024,4096]{1,0:T(8,128)(2,1)} %param.3, f32[4096,128]{1,0:T(8,128)} %all-reduce.11.cloned.1.call-done, f32[4096,128]{1,0:T(8,128)S(1)} %copy-done, f32[128]{0:T(128)S(1)} %div.16, f32[128]{0:T(128)S(1)} %copy-done.6, f32[128]{0:T(128)S(1)} %add_divide_fusion.2, ...), kind=kOutput, calls=%fused_computation.15 | convolution fusion | flops 1077411840 | bytes 13109248 | tf_op jit(solution)/shard_map/dot_general | solution.py:30
  305.4 0.0 all-reduce.13.cloned.1.call-update
  305.4 0.0 all-reduce.15.cloned.1.call-start
  305.4 2.2 multiply_reduce_fusion.2
  307.6 5.9 %psum.109 = f32[128]{0:T(128)S(1)} all-reduce(f32[128]{0:T(128)S(1)} %multiply_reduce_fusion.2), channel_id=1, replica_groups=mesh['samp'=8,'feat'=4] {'feat'}, use_global_device_ids=true, to_apply=%region_13.0 | all-reduce | flops 128 | bytes 1024 | tf_op jit(solution)/shard_map/psum | solution.py:13
  313.6 24.5 %all-reduce.13.cloned.1.call-done = f32[1024,128]{0,1:T(8,128)} async-done(((f32[1024,128]{0,1:T(8,128)}), f32[1024,128]{0,1:T(8,128)}) %all-reduce.13.cloned.1.call-update) | async-done | bytes 524304 | tf_op jit(solution)/shard_map/psum | solution.py:31
  338.1 1.2 multiply_reduce_fusion.6
  339.3 21.4 %psum.108 = f32[128]{0:T(128)S(1)} all-reduce(f32[128]{0:T(128)S(1)} %multiply_reduce_fusion.6), channel_id=1, replica_groups=mesh['samp'=8,'feat'=4] {'samp'}, use_global_device_ids=true, to_apply=%region_11.0 | all-reduce | flops 128 | bytes 1024 | tf_op jit(solution)/shard_map/psum | solution.py:34
  360.6 1.2 multiply_subtract_fusion.3
  361.9 0.8 copy-done.3
  362.7 8.1 %convolution_bitcast_fusion = f32[4096,128]{1,0:T(8,128)} fusion(bf16[1024,4096]{1,0:T(8,128)(2,1)} %param.3, f32[1024,128]{0,1:T(8,128)S(1)} %multiply_subtract_fusion.3), kind=kOutput, calls=%fused_computation | convolution fusion | flops 1073872896 | bytes 11010048 | tf_op jit(solution)/shard_map/dot_general | solution.py:17
  370.7 0.0 all-reduce.15.cloned.1.call-update
  370.8 0.0 all-reduce.17.cloned.1.call-start
  370.8 98.2 %all-reduce.15.cloned.1.call-done = f32[4096,128]{1,0:T(8,128)} async-done(((f32[4096,128]{1,0:T(8,128)}), f32[4096,128]{1,0:T(8,128)}) %all-reduce.15.cloned.1.call-update) | async-done | bytes 2097168 | tf_op jit(solution)/shard_map/psum | solution.py:20
  469.0 3.1 multiply_reduce_fusion.1
  472.0 6.3 %psum.111 = f32[128]{0:T(128)S(1)} all-reduce(f32[128]{0:T(128)S(1)} %multiply_reduce_fusion.1), channel_id=1, replica_groups=mesh['samp'=8,'feat'=4] {'feat'}, use_global_device_ids=true, to_apply=%region_16.0 | all-reduce | flops 128 | bytes 1024 | tf_op jit(solution)/shard_map/psum | solution.py:13
  478.4 3.2 multiply_reduce_fusion
  481.6 1.3 copy-done.1
  482.9 7.1 %convolution_bitcast_fusion.2 = f32[1024,128]{0,1:T(8,128)} fusion(bf16[1024,4096]{1,0:T(8,128)(2,1)} %param.3, f32[4096,128]{1,0:T(8,128)S(1)} %get-tuple-element.5), kind=kOutput, calls=%fused_computation.14 | convolution fusion | flops 1074266112 | bytes 11010048 | tf_op jit(solution)/shard_map/dot_general | solution.py:30
  490.0 0.0 all-reduce.17.cloned.1.call-update
  490.0 5.9 %psum.114 = f32[128]{0:T(128)S(1)} all-reduce(f32[128]{0:T(128)S(1)} %get-tuple-element.4), channel_id=1, replica_groups=mesh['samp'=8,'feat'=4] {'feat'}, use_global_device_ids=true, to_apply=%region_21.0 | all-reduce | flops 128 | bytes 1024 | tf_op jit(solution)/shard_map/psum | solution.py:13
  496.0 26.7 %all-reduce.17.cloned.1.call-done = f32[1024,128]{0,1:T(8,128)} async-done(((f32[1024,128]{0,1:T(8,128)}), f32[1024,128]{0,1:T(8,128)}) %all-reduce.17.cloned.1.call-update) | async-done | bytes 524304 | tf_op jit(solution)/shard_map/psum | solution.py:31
  522.7 1.2 multiply_reduce_fusion.5
  523.9 21.4 %psum.113 = f32[128]{0:T(128)S(1)} all-reduce(f32[128]{0:T(128)S(1)} %multiply_reduce_fusion.5), channel_id=1, replica_groups=mesh['samp'=8,'feat'=4] {'samp'}, use_global_device_ids=true, to_apply=%region_19.0 | all-reduce | flops 128 | bytes 1024 | tf_op jit(solution)/shard_map/psum | solution.py:34
  545.2 1.2 multiply_subtract_fusion.2
  546.4 1.0 copy.8
  547.4 4.2 multiply_add_fusion
  (17 shorter events, 0.1 us)
Async XLA Ops:
  7.2 111.8 %all-reduce.7.cloned.1.call-start = ((), (), s32[]{:S(2)}) async-start(), calls=%async_computation | async-start | bytes 4194304 | tf_op jit(solution)/shard_map/psum | solution.py:20
  14.3 0.7 copy-start.6
  14.4 145.6 %all-reduce.9.cloned.1.call-start = ((), (), s32[]{:S(2)}) async-start(), calls=%async_computation.1 | async-start | bytes 1048576 | tf_op jit(solution)/shard_map/psum | solution.py:31
  15.0 111.9 %copy-start.5 = (f32[1024,128]{1,0:T(8,128)S(1)}, f32[1024,128]{1,0:T(8,128)}, u32[]{:S(2)}) copy-start(f32[1024,128]{1,0:T(8,128)} %param.4) | copy-start | bytes 1572868
  119.0 8.1 %copy-start = (f32[4096,128]{1,0:T(8,128)S(1)}, f32[4096,128]{1,0:T(8,128)}, u32[]{:S(2)}) copy-start(f32[4096,128]{1,0:T(8,128)} %all-reduce.7.cloned.1.call-done) | copy-start | bytes 6291460
  126.9 162.1 %all-reduce.11.cloned.1.call-start = ((), (), s32[]{:S(2)}) async-start(), calls=%async_computation.2 | async-start | bytes 4194304 | tf_op jit(solution)/shard_map/psum | solution.py:20
  190.8 147.3 %all-reduce.13.cloned.1.call-start = ((), (), s32[]{:S(2)}) async-start(), calls=%async_computation.3 | async-start | bytes 1048576 | tf_op jit(solution)/shard_map/psum | solution.py:31
  305.4 55.3 %copy-start.2 = (f32[1024,128]{0,1:T(8,128)S(1)}, f32[1024,128]{0,1:T(8,128)}, u32[]{:S(2)}) copy-start(f32[1024,128]{0,1:T(8,128)} %all-reduce.9.cloned.1.call-done) | copy-start | bytes 1572868
  305.4 163.6 %all-reduce.15.cloned.1.call-start = ((), (), s32[]{:S(2)}) async-start(), calls=%async_computation.4 | async-start | bytes 4194304 | tf_op jit(solution)/shard_map/psum | solution.py:20
  361.9 0.8 copy-start.3
  370.8 151.9 %all-reduce.17.cloned.1.call-start = ((), (), s32[]{:S(2)}) async-start(), calls=%async_computation.5 | async-start | bytes 1048576 | tf_op jit(solution)/shard_map/psum | solution.py:31
  481.6 1.3 copy-start.1
  482.9 62.4 %copy-start.4 = (f32[1024,128]{0,1:T(8,128)S(1)}, f32[1024,128]{0,1:T(8,128)}, u32[]{:S(2)}) copy-start(f32[1024,128]{0,1:T(8,128)} %copy-done.3) | copy-start | bytes 1572868
Sparse Core Ops, SparseCore 0:
  14.5 104.4 all-reduce.6
  127.0 32.8 all-reduce.8
  190.9 98.0 all-reduce.10
  305.5 32.5 all-reduce.12
  370.9 98.0 all-reduce.14
  490.1 32.5 all-reduce.16
where the time goes:
time: 559 us; the launch traced here: 558 us
  waiting for transfers between devices  378 us (68%)
  blocking collectives  95.1 us (17%)
  matrix products  46.2 us (8%)
  other arithmetic  21.3 us (4%)
  between operations  14.2 us (3%)
    psum x3, waiting for transfers between devices, gradient_of(): summed = lax.psum(partial_value, 'samp')  300 us
    psum x3, waiting for transfers between devices, shards(): image = lax.psum(image_partial_value, 'feat')  77.2 us
    psum x3, blocking collectives, shards(): curvature = lax.psum(image_sq, 'samp') + penalty * weight_sum(direction_sq)  64.1 us
    psum x5, blocking collectives, weight_sum(): return lax.psum(value, 'feat')  31 us
    dot_general x3, matrix products, gradient_of(): lax.dot_general(states, residual_b, (((0,), (0,)), ((), ())), preferred_e...  23.5 us
    dot_general x3, matrix products, shards(): jnp.dot(states, direction_b, preferred_element_type=jnp.float32)  22.7 us
  transfers between devices with their start and end apart: 6, of which 6 were waited for; matrix products, arithmetic and copies ran while one was open for 1% of the time, Pallas kernels for 0%

commit v1 on v0

--- a/solution.py
+++ b/solution.py
@@ -28,7 +28,9 @@
     for step in range(ITERS):
         direction_b = direction.astype(jnp.bfloat16)
         image_partial_value = jnp.dot(states, direction_b, preferred_element_type=jnp.float32)
-        image = lax.psum(image_partial_value, "feat")
+        image = image_partial_value
+        for hop in (1, 2):
+            image = image + lax.ppermute(image, "feat", [(dev, dev ^ hop) for dev in range(4)])
         image_sq = jnp.sum(image * image, axis=0)
         direction_sq = jnp.sum(direction * direction, axis=0)
         curvature = lax.psum(image_sq, "samp") + penalty * weight_sum(direction_sq)

time: 559 us -> 513 us (0.918)
  waiting for transfers between devices: 378 us -> 307 us
  blocking collectives: 95.1 us -> 117 us
    psum x3 -> x0, waiting for transfers between devices: 77.2 us -> none  [shards(): image = lax.psum(image_partial_value, 'feat')]
    psum x5, blocking collectives: 31 us -> 57.3 us  [weight_sum(): return lax.psum(value, 'feat')]
    ppermute x0 -> x6, waiting for transfers between devices: none -> 5.7 us  [shards(): lax.ppermute(image, 'feat', [(dev, dev ^ hop) for dev in range(4)])]
  transfers between devices with their start and end apart: 6 -> 9, of which waited for: 6 -> 6; matrix products, arithmetic and copies ran while one was open for 1% -> 0% of each run, Pallas kernels for 0% -> 0%
where the time goes in v1:
time: 513 us
  waiting for transfers between devices  307 us (60%)
  blocking collectives  117 us (23%)
  matrix products  44.3 us (9%)
  other arithmetic  23.2 us (5%)
  between operations  13.9 us (3%)
    psum x3, waiting for transfers between devices, gradient_of(): summed = lax.psum(partial_value, 'samp')  301 us
    psum x3, blocking collectives, shards(): curvature = lax.psum(image_sq, 'samp') + penalty * weight_sum(direction_sq)  60.1 us
    psum x5, blocking collectives, weight_sum(): return lax.psum(value, 'feat')  57.3 us
    dot_general x3, matrix products, gradient_of(): lax.dot_general(states, residual_b, (((0,), (0,)), ((), ())), preferred_e...  23.3 us
    dot_general x3, matrix products, shards(): jnp.dot(states, direction_b, preferred_element_type=jnp.float32)  21 us
  transfers between devices with their start and end apart: 9, of which 6 were waited for; matrix products, arithmetic and copies ran while one was open for 0% of the time, Pallas kernels for 0%

profile of v1, /device:TPU:0, one launch (start us, length us, event | category | flops | bytes accessed | tf_op | source)
XLA Modules:
  0.0 512.6 jit_solution(5344820746191105829)
XLA Ops:
  7.2 0.0 all-reduce.4.cloned.1.call-start
  7.2 7.1 %fusion.5 = f32[4096,128]{1,0:T(8,128)} fusion(bf16[1024,4096]{1,0:T(8,128)(2,1)} %param.3, f32[1024,128]{1,0:T(8,128)} %param.4), kind=kOutput, calls=%fused_computation.28 | convolution fusion | flops 1073872896 | bytes 11010048 | tf_op jit(solution)/shard_map/dot_general | solution.py:17
  14.3 0.0 all-reduce.4.cloned.1.call-update
  14.4 0.0 all-reduce.6.cloned.1.call-start
  14.4 0.6 copy-done.6
  15.0 104.0 %all-reduce.4.cloned.1.call-done = f32[4096,128]{1,0:T(8,128)} async-done(((f32[4096,128]{1,0:T(8,128)}), f32[4096,128]{1,0:T(8,128)}) %all-reduce.4.cloned.1.call-update) | async-done | bytes 2097168 | tf_op jit(solution)/shard_map/psum | solution.py:20
  119.0 6.9 %convolution_bitcast_fusion.4 = f32[1024,128]{0,1:T(8,128)S(1)} fusion(bf16[1024,4096]{1,0:T(8,128)(2,1)} %param.3, f32[4096,128]{1,0:T(8,128)} %all-reduce.4.cloned.1.call-done, f32[128]{0:T(128)S(1)} %broadcast_multiply_fusion), kind=kOutput, calls=%fused_computation.16 | convolution fusion | flops 1074790400 | bytes 11010560 | tf_op jit(solution)/shard_map/dot_general | solution.py:30
  125.9 0.1 collective-permute-start
  126.0 1.9 collective-permute-done
  127.9 0.9 add.62
  128.8 1.5 collective-permute-start.1
  130.2 0.2 copy.5
  130.5 0.6 multiply_reduce_fusion.4
  131.0 14.6 %psum.81 = f32[128]{0:T(128)S(1)} all-reduce(f32[128]{0:T(128)S(1)} %multiply_reduce_fusion.4), channel_id=1, replica_groups=mesh['samp'=8,'feat'=4] {'feat'}, use_global_device_ids=true, to_apply=%region_2.0 | all-reduce | flops 128 | bytes 1024 | tf_op jit(solution)/shard_map/psum | solution.py:13
  145.6 1.3 multiply_reduce_fusion.7
  146.9 20.0 %psum.82 = f32[128]{0:T(128)S(1)} all-reduce(f32[128]{0:T(128)S(1)} %get-tuple-element.10), channel_id=1, replica_groups=mesh['samp'=8,'feat'=4] {'samp'}, use_global_device_ids=true, to_apply=%region_4.0 | all-reduce | flops 128 | bytes 1024 | tf_op jit(solution)/shard_map/psum | solution.py:36
  167.0 8.1 %convolution_bitcast_fusion.1 = f32[4096,128]{1,0:T(8,128)} fusion(bf16[1024,4096]{1,0:T(8,128)(2,1)} %param.3, f32[1024,128]{0,1:T(8,128)S(1)} %copy.5, f32[1024,128]{0,1:T(8,128)S(1)} %get-tuple-element.11, f32[128]{0:T(128)S(1)} %add_divide_fusion.2), kind=kOutput, calls=%fused_computation.1 | convolution fusion | flops 1074135040 | bytes 11534848 | tf_op jit(solution)/shard_map/dot_general | solution.py:17
  175.1 0.0 all-reduce.8.cloned.1.call-start
  175.2 98.2 %all-reduce.6.cloned.1.call-done = f32[4096,128]{1,0:T(8,128)} async-done(((f32[4096,128]{1,0:T(8,128)}), f32[4096,128]{1,0:T(8,128)}) %all-reduce.6.cloned.1.call-update) | async-done | bytes 2097168 | tf_op jit(solution)/shard_map/psum | solution.py:20
  273.4 2.2 multiply_reduce_fusion.3
  275.5 6.5 %psum.84 = f32[128]{0:T(128)S(1)} all-reduce(f32[128]{0:T(128)S(1)} %multiply_reduce_fusion.3), channel_id=1, replica_groups=mesh['samp'=8,'feat'=4] {'feat'}, use_global_device_ids=true, to_apply=%region_7.0 | all-reduce | flops 128 | bytes 1024 | tf_op jit(solution)/shard_map/psum | solution.py:13
  282.0 7.1 %convolution_bitcast_fusion.3 = f32[1024,128]{0,1:T(8,128)S(1)} fusion(bf16[1024,4096]{1,0:T(8,128)(2,1)} %param.3, f32[4096,128]{1,0:T(8,128)} %all-reduce.6.cloned.1.call-done, f32[4096,128]{1,0:T(8,128)S(1)} %copy-done, f32[128]{0:T(128)S(1)} %div.16, f32[128]{0:T(128)S(1)} %copy-done.6, f32[128]{0:T(128)S(1)} %add_divide_fusion.2, ...), kind=kOutput, calls=%fused_computation.15 | convolution fusion | flops 1077411840 | bytes 13109248 | tf_op jit(solution)/shard_map/dot_general | solution.py:30
  289.1 0.1 collective-permute-start.2
  289.2 1.9 collective-permute-done.2
  291.1 0.9 add.66
  291.9 1.1 collective-permute-start.3
  293.0 0.6 multiply_reduce_fusion.2
  293.6 14.8 %psum.86 = f32[128]{0:T(128)S(1)} all-reduce(f32[128]{0:T(128)S(1)} %multiply_reduce_fusion.2), channel_id=1, replica_groups=mesh['samp'=8,'feat'=4] {'feat'}, use_global_device_ids=true, to_apply=%region_11.0 | all-reduce | flops 128 | bytes 1024 | tf_op jit(solution)/shard_map/psum | solution.py:13
  308.3 2.1 multiply_reduce_fusion.6
  310.4 20.0 %psum.85 = f32[128]{0:T(128)S(1)} all-reduce(f32[128]{0:T(128)S(1)} %get-tuple-element.8), channel_id=1, replica_groups=mesh['samp'=8,'feat'=4] {'samp'}, use_global_device_ids=true, to_apply=%region_9.0 | all-reduce | flops 128 | bytes 1024 | tf_op jit(solution)/shard_map/psum | solution.py:36
  330.4 1.2 multiply_subtract_fusion.3
  331.7 0.8 copy-done.3
  332.5 8.1 %convolution_bitcast_fusion = f32[4096,128]{1,0:T(8,128)} fusion(bf16[1024,4096]{1,0:T(8,128)(2,1)} %param.3, f32[1024,128]{0,1:T(8,128)S(1)} %multiply_subtract_fusion.3), kind=kOutput, calls=%fused_computation | convolution fusion | flops 1073872896 | bytes 11010048 | tf_op jit(solution)/shard_map/dot_general | solution.py:17
  340.6 99.3 %all-reduce.8.cloned.1.call-done = f32[4096,128]{1,0:T(8,128)} async-done(((f32[4096,128]{1,0:T(8,128)}), f32[4096,128]{1,0:T(8,128)}) %all-reduce.8.cloned.1.call-update) | async-done | bytes 2097168 | tf_op jit(solution)/shard_map/psum | solution.py:20
  439.8 3.1 multiply_reduce_fusion.1
  442.9 6.3 %psum.88 = f32[128]{0:T(128)S(1)} all-reduce(f32[128]{0:T(128)S(1)} %multiply_reduce_fusion.1), channel_id=1, replica_groups=mesh['samp'=8,'feat'=4] {'feat'}, use_global_device_ids=true, to_apply=%region_14.0 | all-reduce | flops 128 | bytes 1024 | tf_op jit(solution)/shard_map/psum | solution.py:13
  449.2 3.2 multiply_reduce_fusion
  452.4 7.0 %convolution_bitcast_fusion.2 = f32[1024,128]{0,1:T(8,128)S(1)} fusion(bf16[1024,4096]{1,0:T(8,128)(2,1)} %param.3, f32[4096,128]{1,0:T(8,128)S(1)} %get-tuple-element.5), kind=kOutput, calls=%fused_computation.14 | convolution fusion | flops 1074266112 | bytes 11010048 | tf_op jit(solution)/shard_map/dot_general | solution.py:30
  459.5 0.1 collective-permute-start.4
  459.5 1.9 collective-permute-done.4
  461.4 0.1 add.71
  461.5 1.1 collective-permute-start.5
  462.6 15.1 %psum.90 = f32[128]{0:T(128)S(1)} all-reduce(f32[128]{0:T(128)S(1)} %get-tuple-element.4), channel_id=1, replica_groups=mesh['samp'=8,'feat'=4] {'feat'}, use_global_device_ids=true, to_apply=%region_18.0 | all-reduce | flops 128 | bytes 1024 | tf_op jit(solution)/shard_map/psum | solution.py:13
  477.8 1.9 multiply_reduce_fusion.5
  479.7 20.0 %psum.89 = f32[128]{0:T(128)S(1)} all-reduce(f32[128]{0:T(128)S(1)} %get-tuple-element.6), channel_id=1, replica_groups=mesh['samp'=8,'feat'=4] {'samp'}, use_global_device_ids=true, to_apply=%region_16.0 | all-reduce | flops 128 | bytes 1024 | tf_op jit(solution)/shard_map/psum | solution.py:36
  499.7 1.2 multiply_subtract_fusion.2
  500.9 1.0 copy.8
  501.9 4.2 multiply_add_fusion
  (23 shorter events, 0.1 us)
Async XLA Ops:
  7.2 111.8 %all-reduce.4.cloned.1.call-start = ((), (), s32[]{:S(2)}) async-start(), calls=%async_computation | async-start | bytes 4194304 | tf_op jit(solution)/shard_map/psum | solution.py:20
  14.3 0.7 copy-start.6
  14.4 259.0 %all-reduce.6.cloned.1.call-start = ((), (), s32[]{:S(2)}) async-start(), calls=%async_computation.1 | async-start | bytes 4194304 | tf_op jit(solution)/shard_map/psum | solution.py:20
  15.0 115.2 %copy-start.5 = (f32[1024,128]{1,0:T(8,128)S(1)}, f32[1024,128]{1,0:T(8,128)}, u32[]{:S(2)}) copy-start(f32[1024,128]{1,0:T(8,128)} %param.4) | copy-start | bytes 1572868
  125.9 4.5 copy-start
  125.9 2.0 collective-permute-start
  128.8 16.8 %collective-permute-start.1 = (f32[1024,128]{0,1:T(8,128)}, f32[1024,128]{0,1:T(8,128)}, u32[]{:S(2)}, u32[]{:S(2)}) collective-permute-start(f32[1024,128]{0,1:T(8,128)} %add.62), channel_id=1, source_target_pairs={{0,2},{1,3},{2,0},{3,1},{4,6},{5,7},{6,4},{7,5},{8,10},{9,11},{10,... | collective-permute-start | bytes 1572872 | tf_op jit(solution)/shard_map/ppermute | solution.py:33
  175.1 264.7 %all-reduce.8.cloned.1.call-start = ((), (), s32[]{:S(2)}) async-start(), calls=%async_computation.2 | async-start | bytes 4194304 | tf_op jit(solution)/shard_map/psum | solution.py:20
  282.0 11.0 %copy-start.1 = (f32[4096,128]{1,0:T(8,128)S(1)}, f32[4096,128]{1,0:T(8,128)}, u32[]{:S(2)}) copy-start(f32[4096,128]{1,0:T(8,128)} %all-reduce.6.cloned.1.call-done) | copy-start | bytes 6291460
  289.1 2.0 collective-permute-start.2
  291.9 16.4 %collective-permute-start.3 = (f32[1024,128]{0,1:T(8,128)}, f32[1024,128]{0,1:T(8,128)}, u32[]{:S(2)}, u32[]{:S(2)}) collective-permute-start(f32[1024,128]{0,1:T(8,128)} %add.66), channel_id=1, source_target_pairs={{0,2},{1,3},{2,0},{3,1},{4,6},{5,7},{6,4},{7,5},{8,10},{9,11},{10,... | collective-permute-start | bytes 1572872 | tf_op jit(solution)/shard_map/ppermute | solution.py:33
  331.7 0.8 copy-start.3
  452.4 7.0 %copy-start.2 = (f32[4096,128]{1,0:T(8,128)}, f32[4096,128]{1,0:T(8,128)S(1)}, u32[]{:S(2)}) copy-start(f32[4096,128]{1,0:T(8,128)S(1)} %get-tuple-element.5) | copy-start | bytes 6291460
  459.5 40.3 %copy-start.4 = (f32[1024,128]{0,1:T(8,128)S(1)}, f32[1024,128]{0,1:T(8,128)}, u32[]{:S(2)}) copy-start(f32[1024,128]{0,1:T(8,128)} %copy-done.3) | copy-start | bytes 1572868
  459.5 2.0 collective-permute-start.4
  461.5 16.3 %collective-permute-start.5 = (f32[1024,128]{0,1:T(8,128)S(1)}, f32[1024,128]{0,1:T(8,128)}, u32[]{:S(2)}, u32[]{:S(2)}) collective-permute-start(f32[1024,128]{0,1:T(8,128)S(1)} %add.71), channel_id=1, source_target_pairs={{0,2},{1,3},{2,0},{3,1},{4,6},{5,7},{6,4},{7,5},{8,10},{9,11},{10,... | collective-permute-start | bytes 1572872 | tf_op jit(solution)/shard_map/ppermute | solution.py:33
Sparse Core Ops, SparseCore 0:
  14.5 104.4 all-reduce.3
  175.2 98.0 all-reduce.5
  340.7 99.0 all-reduce.7
